TPU v7x, 512 devices: a whole 4x4x16 slice. The times are simulated.
512 devices in a mesh: tm: 64 (over z, x), chan: 8 (over y, core).
Axes of the slice: x: 4, y: 4, z: 16, core: 2. Of those that a mesh axis runs over, the one named last changes fastest.
Arguments:
- observations: bfloat16 [8, 512, 4096], P(None, 'tm', 'chan'), may hold values from -6 to 6
- obs_matrix: bfloat16 [4096, 512], P('chan'), may hold values from -0.125 to 0.125
- block_pattern: int32 [32, 4], P('chan'), may hold values 0 or 1
- noise_precision: float32 [4096], P('chan'), may hold values from 0.25 to 4
- retention: float32 [8, 512], replicated, may hold values from 0.25 to 1
- prior_mean: float32 [512], replicated, may hold values from -6 to 6
- filter_matrix: float32 [512, 512], replicated, may hold values from -1 to 1, as said below
- filter_gain: float32 [512, 512], replicated, may hold values from -0.0234375 to 0.0234375
- transition: float32 [512, 512], replicated, may hold values from -0.25 to 0.25
- smoother_gain: float32 [512, 512], replicated, may hold values from -1 to 1, as said below
Outputs:
- filtered: float32 [8, 512, 512], P(None, 'tm', 'chan')
- smoothed: float32 [8, 512, 512], P(None, 'tm', 'chan')
Inputs may be any that keep to these rules, and one draw needn't show every extreme that they name: `filter_matrix`: spectral norm below 1. `smoother_gain`: spectral norm below 1.
All inputs are finite; a program needn't handle non-finite values. No bound on the sum of `block_pattern` on one device may be relied on, other than what follows from the above.
Results may differ from a plain program's by a relative error of at most 0.0027.
Values sent between devices are 32-bit elements; how exact they have to be, the bound alone decides.
A program may use at most 64 MiB of HBM per device.

v0:
```python
import jax
import jax.numpy as jnp
from jax import lax
from jax.sharding import PartitionSpec as P

BLOCK = 128


def from_behind(block, axis, distance):
    devices = range(lax.axis_size(axis))
    route = [(i - distance, i) for i in devices if i - distance in devices]
    return lax.ppermute(block, axis, route)


def product(left, right):
    return jnp.dot(left, right, precision=lax.Precision.HIGHEST, preferred_element_type=jnp.float32)


def matrix_power(matrix, exponent):
    result = None
    squared = matrix
    while exponent:
        if exponent & 1:
            result = squared
        exponent = exponent >> 1
        if exponent:
            squared = product(squared, squared)
    return result


def run_filter(start, retained, driving, filter_matrix):

    def advance(loop_state, inputs):
        retain_now, forcing = inputs
        loop_state = retain_now[:, None] * product(loop_state, filter_matrix) + forcing
        return (loop_state, loop_state)

    final_state, states = lax.scan(
        advance, start, (jnp.swapaxes(retained, 0, 1), jnp.swapaxes(driving, 0, 1))
    )
    return (jnp.swapaxes(states, 0, 1), final_state)


def run_smoother(start, correction, smoother_gain):

    def retreat(loop_state, forcing):
        loop_state = product(loop_state, smoother_gain) + forcing
        return (loop_state, loop_state)

    first_state, states = lax.scan(retreat, start, jnp.swapaxes(correction, 0, 1), reverse=True)
    return (jnp.swapaxes(states, 0, 1), first_state)


def per_device(
    observations,
    obs_matrix,
    block_pattern,
    noise_precision,
    retention,
    prior_mean,
    filter_matrix,
    filter_gain,
    transition,
    smoother_gain,
):
    position = lax.axis_index("tm")
    device_count = lax.axis_size("tm")
    column_index = lax.axis_index("chan")
    chan_count = lax.axis_size("chan")
    series, step_count, channels = observations.shape
    state_width = obs_matrix.shape[1]
    block_mask = jnp.repeat(jnp.repeat(block_pattern, BLOCK, axis=0), BLOCK, axis=1).astype(
        jnp.bfloat16
    )
    obs_used = obs_matrix * block_mask
    weighted = (observations.astype(jnp.float32) * noise_precision).astype(jnp.bfloat16)
    partial_value = jnp.dot(
        weighted.reshape(series * step_count, channels),
        obs_used,
        preferred_element_type=jnp.float32,
    )
    information = lax.psum(partial_value, "chan")
    driving = product(information, filter_gain).reshape(series, step_count, state_width)
    retained = lax.dynamic_slice_in_dim(retention, position * step_count, step_count, 1)
    first_device = position == 0
    last_device = position == device_count - 1
    prior_rows = jnp.broadcast_to(prior_mean, (series, state_width))
    opening_state = jnp.where(first_device, prior_rows, 0.0)
    _, local_end = run_filter(opening_state, retained, driving, filter_matrix)
    block_gain = jnp.prod(retained, axis=1)[:, None]
    forward_power = matrix_power(filter_matrix, step_count)

    def forward_turn(turn_index, loop_state):
        shifted, ending = loop_state
        shifted = from_behind(ending, "tm", 1)
        ending = lax.cond(
            position == turn_index,
            lambda: block_gain * product(shifted, forward_power) + local_end,
            lambda: ending,
        )
        return (shifted, ending)

    shifted, _ = lax.fori_loop(1, device_count, forward_turn, (local_end, local_end))
    carry_in = jnp.where(first_device, prior_rows, shifted)
    filtered_rows, _ = run_filter(carry_in, retained, driving, filter_matrix)
    predicted = product(filtered_rows.reshape(series * step_count, state_width), transition)
    correction = filtered_rows - product(predicted, smoother_gain).reshape(
        series, step_count, state_width
    )
    boundary = predicted.reshape(series, step_count, state_width)[:, step_count - 1, :]
    finish = jnp.where(last_device, boundary, 0.0)
    _, local_first = run_smoother(finish, correction, smoother_gain)
    backward_power = matrix_power(smoother_gain, step_count)

    def backward_turn(turn_index, loop_state):
        shifted_back, opening = loop_state
        shifted_back = from_behind(opening, "tm", -1)
        opening = lax.cond(
            position == device_count - 1 - turn_index,
            lambda: product(shifted_back, backward_power) + local_first,
            lambda: opening,
        )
        return (shifted_back, opening)

    shifted_back, _ = lax.fori_loop(1, device_count, backward_turn, (local_first, local_first))
    carry_back = jnp.where(last_device, boundary, shifted_back)
    smoothed_rows, _ = run_smoother(carry_back, correction, smoother_gain)
    column_width = state_width // chan_count
    filtered = lax.dynamic_slice_in_dim(filtered_rows, column_index * column_width, column_width, 2)
    smoothed = lax.dynamic_slice_in_dim(smoothed_rows, column_index * column_width, column_width, 2)
    return (filtered, smoothed)


def solution(mesh):
    placed = (
        P(None, "tm", "chan"),
        P("chan", None),
        P("chan", None),
        P("chan"),
        P(),
        P(),
        P(),
        P(),
        P(),
        P(),
    )
    return jax.shard_map(
        per_device,
        mesh=mesh,
        in_specs=placed,
        out_specs=(P(None, "tm", "chan"), P(None, "tm", "chan")),
        check_vma=False,
    )
```

profile of v0, /device:TPU:102, one launch (start us, length us, event | category | flops | bytes accessed | tf_op | source)
XLA Modules:
  0.0 1267.3 jit_solution(12299530745839275318)
XLA Ops:
  24.5 63.9 %all-reduce.2.cloned.1.call-done = f32[64,512]{1,0:T(8,128)} async-done(((f32[64,512]{1,0:T(8,128)}), f32[64,512]{1,0:T(8,128)}) %all-reduce.2.cloned.1.call-update) | async-done | bytes 131088 | tf_op jit(solution)/shard_map/psum | solution.py:82
  96.1 569.3 %while.89 = (s32[]{:T(128)}, f32[8,512]{1,0:T(8,128)}, f32[8,512]{1,0:T(8,128)S(1)}, s32[]{:T(128)}, f32[8,1]{0,1:T(1,128)S(1)}, /*index=5*/f32[512,512]{1,0:T(8,128)}, f32[8,512]{1,0:T(8,128)S(1)}, s32[]{:T(128)}) while((s32[]{:T(128)}, f32[8,512]{1,0:T(8,128)}, f32[8,512]{1,0:T(8,128)S(1)}, s32[]{:T(128)}, f32[8,1]{0,1:T(1,128)S(1)}, ...), condition=%wide.region_7.8_spmd, body=%wide.region_4.7_spmd.sunk | while | flops 25174020 | bytes 1163475 | solution.py:103
  102.2 7.6 collective-permute-start
  111.2 7.6 collective-permute-start
  120.2 7.6 collective-permute-start
  138.3 7.7 collective-permute-start
  156.5 7.6 collective-permute-start
  165.6 7.6 collective-permute-start
  174.6 7.6 collective-permute-start
  183.7 7.6 collective-permute-start
  201.8 7.6 collective-permute-start
  219.9 7.6 collective-permute-start
  238.0 9.5 collective-permute-start
  248.9 7.6 collective-permute-start
  267.0 7.6 collective-permute-start
  276.1 7.6 collective-permute-start
  285.1 7.6 collective-permute-start
  303.2 7.6 collective-permute-start
  312.3 7.6 collective-permute-start
  330.4 7.6 collective-permute-start
  339.5 7.6 collective-permute-start
  348.5 7.6 collective-permute-start
  366.6 7.6 collective-permute-start
  375.7 7.6 collective-permute-start
  393.8 7.6 collective-permute-start
  402.8 7.6 collective-permute-start
  411.9 7.6 collective-permute-start
  430.0 7.6 collective-permute-start
  457.1 7.6 collective-permute-start
  520.5 7.6 collective-permute-start
  583.9 7.6 collective-permute-start
  680.9 571.9 %while.92 = (s32[]{:T(128)}, f32[8,512]{1,0:T(8,128)}, f32[8,512]{1,0:T(8,128)S(1)}, s32[]{:T(128)}, f32[512,512]{1,0:T(8,128)S(1)}, /*index=5*/f32[8,512]{1,0:T(8,128)S(1)}, s32[]{:T(128)}, s32[]{:T(128)}) while((s32[]{:T(128)}, f32[8,512]{1,0:T(8,128)}, f32[8,512]{1,0:T(8,128)S(1)}, s32[]{:T(128)}, f32[512,512]{1,0:T(8,128)S(1)}, ...), condition=%wide.region_15.16_spmd, body=%wide.region_12.15_spmd.sunk | while | flops 25169924 | bytes 1163447 | solution.py:125
  (515 shorter events, 989.1 us)
Async XLA Ops:
  7.2 81.2 %all-reduce.2.cloned.1.call-start = ((), (), s32[]{:S(2)}) async-start(), calls=%async_computation | async-start | bytes 262144 | tf_op jit(solution)/shard_map/psum | solution.py:82
  102.2 9.0 collective-permute-start
  120.2 9.0 collective-permute-start
  138.3 9.1 collective-permute-start
  165.6 9.0 collective-permute-start
  183.7 9.0 collective-permute-start
  201.8 9.1 collective-permute-start
  238.0 10.9 collective-permute-start
  248.9 9.0 collective-permute-start
  267.0 9.1 collective-permute-start
  285.1 9.0 collective-permute-start
  312.3 9.0 collective-permute-start
  330.4 9.1 collective-permute-start
  348.5 9.0 collective-permute-start
  375.7 9.0 collective-permute-start
  393.8 9.1 collective-permute-start
  411.9 9.0 collective-permute-start
  439.0 9.0 collective-permute-start
  457.1 9.1 collective-permute-start
  475.2 9.0 collective-permute-start
  502.4 9.0 collective-permute-start
  520.5 9.1 collective-permute-start
  538.6 9.0 collective-permute-start
  565.8 9.0 collective-permute-start
  583.9 9.1 collective-permute-start
  602.0 9.0 collective-permute-start
  680.9 9.4 collective-permute-start.1
  780.8 9.1 collective-permute-start.1
  844.2 9.1 collective-permute-start.1
  907.5 9.1 collective-permute-start.1
  970.9 9.1 collective-permute-start.1
  1117.0 9.1 collective-permute-start.1
  (103 other events, 950.1 us)
Sparse Core Ops, SparseCore 0:
  10.3 78.0 all-reduce.1
where the time goes:
time: 1270 us
  waiting for transfers between devices  602 us (47%)
  starting transfers between devices  598 us (47%)
  matrix products  40.7 us (3%)
  between operations  14.2 us (1%)
    ppermute x126, starting transfers between devices, from_behind(): return lax.ppermute(block, axis, route)  598 us
    ppermute x126, waiting for transfers between devices, from_behind(): return lax.ppermute(block, axis, route)  538 us
    psum x1, waiting for transfers between devices, per_device(): information = lax.psum(partial_value, 'chan')  63.9 us
    dot_general x43, matrix products, product(): jnp.dot(left, right, precision=lax.Precision.HIGHEST, preferred_element_t...  39.8 us
  transfers between devices with their start and end apart: 127, of which 127 were waited for; matrix products, arithmetic and copies ran while one was open for 1% of the time, Pallas kernels for 0%

commit v1 on v0

v1 whole, which is shorter than its diff:
```python
import functools

import jax
import jax.numpy as jnp
from jax import lax
from jax.experimental import pallas as pl
from jax.experimental.pallas import tpu as pltpu
from jax.sharding import PartitionSpec as P

BLOCK = 128
PLANE = 4
MESH = pl.DeviceIdType.MESH
f32 = jnp.float32
bf16 = jnp.bfloat16


def dot(a, b):
    return jnp.dot(a, b, preferred_element_type=f32)


def split(x):
    high = x.astype(bf16)
    return high, (x - high.astype(f32)).astype(bf16)


def times(x, high, low):
    rows = x.shape[0]
    if rows % 16:
        x_high = x.astype(bf16).astype(f32)
        both = jnp.concatenate([x_high, x - x_high], 0).astype(bf16)
        first, second = dot(both, high), dot(both, low)
        return first[:rows] + (first[rows:] + second[:rows])
    x_high, x_low = split(x)
    if rows >= 256:
        return dot(x_high, high) + (dot(x_low, high) + dot(x_high, low))
    first = dot(jnp.concatenate([x_high, x_low], 0), high)
    return first[:rows] + (first[rows:] + dot(x_high, low))


def shifted(x, distance):
    return jnp.roll(x, distance, axis=0)


def kernel(
    nx, nz, nc, steps, width, channels,
    obs_hbm, mat_hbm, pattern, noise, retention, prior, f_hbm, k_hbm, t_hbm, g_hbm,
    filtered, smoothed,
    obs, mat, raw, fh, fl, gh, gl, wh, wl, kh, kl,
    part, part_in, drive, ends, starts, rho, rows_y, rows_c, fbuf, cbuf, bbuf,
    out_f, out_s, in_f, in_s,
    load_sem, rs_send, rs_recv, x_send, x_recv, e_send, e_recv, b_send, b_recv,
    of_send, of_recv, os_send, os_recv,
):
    tm, chan = lax.axis_index("tm"), lax.axis_index("chan")
    z, x = tm // nx, tm % nx
    span = nx * steps
    total = nz * span
    local_bits = span.bit_length() - 1
    z_bits = nz.bit_length() - 1

    loads = [
        pltpu.make_async_copy(source, target, load_sem.at[i])
        for i, (source, target) in enumerate(
            (
                (mat_hbm, mat),
                (obs_hbm, obs),
                (f_hbm, raw.at[0]),
                (k_hbm, raw.at[1]),
                (g_hbm, raw.at[2]),
                (t_hbm, raw.at[3]),
            )
        )
    ]
    for load in loads:
        load.start()

    def chan_peer(i):
        return {"chan": lax.rem(chan + i, nc)}

    def x_peer(i):
        return {"tm": z * nx + lax.rem(x + i, nx)}

    def z_peer(i):
        return {"tm": lax.rem(z + i, nz) * nx + x}

    barrier = pltpu.get_barrier_semaphore()
    for i in range(1, nz):
        pl.semaphore_signal(barrier, inc=1, device_id=z_peer(i), device_id_type=MESH)
    for i in range(1, nx):
        pl.semaphore_signal(barrier, inc=1, device_id=x_peer(i), device_id_type=MESH)
    for i in range(1, nc):
        pl.semaphore_signal(barrier, inc=1, device_id=chan_peer(i), device_id_type=MESH)

    def remote(source, target, send, recv, peer):
        return pltpu.make_async_remote_copy(
            src_ref=source, dst_ref=target, send_sem=send, recv_sem=recv,
            device_id=peer, device_id_type=MESH,
        )

    def square(high, low, first, last):
        def body(i, _):
            a, b = high[i], low[i]
            h, l = split(dot(a, a) + (dot(a, b) + dot(b, a)))
            high[i + 1] = h
            low[i + 1] = l
            return 0

        lax.fori_loop(first, last, body, 0)

    loads[0].wait()
    loads[1].wait()
    weighted = obs[...].astype(f32) * noise[...].reshape(1, 1, channels)
    weighted = weighted.reshape(nc * steps, channels).astype(bf16)
    lane_block = lax.broadcasted_iota(jnp.int32, (BLOCK, width), 1) // BLOCK
    used = []
    for i in range(channels // BLOCK):
        mask = jnp.zeros((BLOCK, width), f32)
        for j in range(width // BLOCK):
            mask = jnp.where(lane_block == j, pattern[i, j].astype(f32), mask)
        used.append(mat[i * BLOCK : (i + 1) * BLOCK] * mask.astype(bf16))
    part[...] = dot(weighted, jnp.concatenate(used, 0)).reshape(nc, steps, width)

    loads[2].wait()
    fh[0], fl[0] = split(raw[0])
    square(fh, fl, 0, 2)

    pl.semaphore_wait(barrier, nz + nx + nc - 3)
    sums = []
    for i in range(1, nc):
        there = lax.rem(chan + i, nc)
        copy = remote(part.at[there], part_in.at[chan], rs_send.at[i], rs_recv.at[i], chan_peer(i))
        copy.start()
        sums.append(copy)
    part_in[chan] = part[chan]

    row = retention[pl.ds(chan, 1), :]
    here = lax.broadcasted_iota(jnp.int32, (total, total), 0)
    there = lax.broadcasted_iota(jnp.int32, (total, total), 1)
    picked = jnp.where(there == (here % nz) * span + here // nz, row, 0.0)
    column = jnp.sum(picked, axis=1, keepdims=True)
    running = column[:nz]
    rho[:nz] = running
    for t in range(1, span):
        running = running * column[t * nz : (t + 1) * nz]
        rho[t * nz : (t + 1) * nz] = running
    block_row = lax.broadcasted_iota(jnp.int32, (nz, 1), 0)
    chain = jnp.where(block_row >= 1, shifted(running, 1), 0.0)
    block_factors = [chain]
    for level in range(1, z_bits):
        chain = chain * shifted(chain, 1 << (level - 1))
        block_factors.append(jnp.where(block_row >= (1 << level), chain, 0.0))
    step_row = lax.broadcasted_iota(jnp.int32, (span, 1), 0)
    here = lax.broadcasted_iota(jnp.int32, (span, total), 0)
    there = lax.broadcasted_iota(jnp.int32, (span, total), 1)
    own = jnp.sum(jnp.where(there == here + z * span, row, 0.0), axis=1, keepdims=True)
    own_factors = [jnp.where(step_row >= 1, own, 0.0)]
    for level in range(1, local_bits):
        own = own * shifted(own, 1 << (level - 1))
        own_factors.append(jnp.where(step_row >= (1 << level), own, 0.0))

    loads[3].wait()
    kh[...], kl[...] = split(raw[1])
    square(fh, fl, 2, local_bits)

    for copy in sums:
        copy.wait()
    information = part_in[0]
    for i in range(1, nc):
        information = information + part_in[i]
    drive[x] = times(information, kh[...], kl[...])
    spread = []
    for i in range(1, nx):
        copy = remote(drive.at[x], drive.at[x], x_send.at[i], x_recv.at[i], x_peer(i))
        copy.start()
        spread.append(copy)

    loads[4].wait()
    loads[5].wait()
    gh[0], gl[0] = split(raw[2])
    th, tl = split(raw[3])
    eye = lax.broadcasted_iota(jnp.int32, (width, width), 0) == lax.broadcasted_iota(
        jnp.int32, (width, width), 1
    )
    product = dot(th, gh[0]) + (dot(th, gl[0]) + dot(tl, gh[0]))
    wh[...], wl[...] = split(jnp.where(eye, 1.0, 0.0) - product)
    square(gh, gl, 0, 3)

    for copy in spread:
        copy.wait()

    local = drive[...].reshape(span, width)
    for level in range(local_bits):
        moved = shifted(local, 1 << level)
        local = local + own_factors[level] * times(moved, fh[level], fl[level])
    ends[z] = local[span - 1 :]
    across = []
    for i in sorted(range(1, nz), key=lambda i: -min(i, nz - i)):
        copy = remote(ends.at[z], ends.at[z], e_send.at[i], e_recv.at[i], z_peer(i))
        copy.start()
        across.append(copy)

    square(gh, gl, 3, 4)
    last_plane = z == nz - 1
    corrected = times(local, wh[...], wl[...])
    corrected = jnp.where(last_plane & (step_row == span - 1), local, corrected)
    backward = corrected
    for level in (2, 1, 0):
        backward = backward + times(shifted(backward, -(1 << level)), gh[level], gl[level])
    bbuf[...] = backward.reshape(nx, steps, width)
    for level in range(local_bits - 1, 2, -1):
        backward = backward + times(shifted(backward, -(1 << level)), gh[level], gl[level])
    starts[z] = backward[:1]
    for i in sorted(range(1, nz), key=lambda i: -min(i, nz - i)):
        copy = remote(starts.at[z], starts.at[z], b_send.at[i], b_recv.at[i], z_peer(i))
        copy.start()
        across.append(copy)

    square(fh, fl, local_bits, local_bits + z_bits - 1)
    square(gh, gl, 4, local_bits + z_bits - 1)

    for copy in across[: nz - 1]:
        copy.wait()

    carry = jnp.where(block_row == 0, prior[...], shifted(ends[...].reshape(nz, width), 1))
    for level in range(z_bits):
        moved = shifted(carry, 1 << level)
        high, low = fh[local_bits + level], fl[local_bits + level]
        carry = carry + block_factors[level] * times(moved, high, low)

    rows_y[:nz] = times(carry, fh[0], fl[0])
    for level in range(local_bits):
        count = nz << level
        rows_y[count : 2 * count] = times(rows_y[:count], fh[level], fl[level])
    scaled = rows_y[...] * rho[...]
    is_own = lax.broadcasted_iota(jnp.int32, (1, nz, 1), 1) == z
    picked = jnp.sum(jnp.where(is_own, scaled.reshape(span, nz, width), 0.0), axis=1)
    fbuf[...] = (local + picked).reshape(nx, steps, width)

    def send_out(state, out, into, send, recv):
        copies = []
        for k in range(width // BLOCK):
            out[k] = state[:, k * BLOCK : (k + 1) * BLOCK]
        for i in range(1, nc):
            there = lax.rem(chan + i, nc)
            copy = remote(out.at[there // 2], into.at[chan], send.at[i], recv.at[i], chan_peer(i))
            copy.start()
            copies.append(copy)
        into[chan] = out[chan // 2]
        return copies

    copies_f = send_out(fbuf[x], out_f, in_f, of_send, of_recv)

    turned = times(rows_y[...] * rho[...], wh[...], wl[...])
    final = lax.broadcasted_iota(jnp.int32, (total, 1), 0) == total - 1
    turned = jnp.where(final, rows_y[...] * rho[...], turned)
    rows_c[...] = turned.reshape(nx, steps, nz, width)
    for t in range(span):
        row = rows_c[t // steps, t % steps]
        row = jnp.sum(jnp.where(block_row == z, row, 0.0), axis=0, keepdims=True)
        cbuf[t // steps, t % steps : t % steps + 1] = row
    cbuf[...] = cbuf[...] + corrected.reshape(nx, steps, width)

    for level in (2, 1, 0):
        half = 1 << level
        few = max(1, min(nx, 128 // (half * nz)))

        def reduce_rows(i, _):
            q = pl.ds(i * few, few)
            upper = rows_c[q, half : 2 * half].reshape(few * half * nz, width)
            upper = times(upper, gh[level], gl[level]).reshape(few, half, nz, width)
            rows_c[q, :half] = rows_c[q, :half] + upper
            return 0

        lax.fori_loop(0, nx // few, reduce_rows, 0)

    for copy in across[nz - 1 :]:
        copy.wait()
    whole = block_row == z
    for q in range(nx):
        own_start = bbuf[q][:1]
        if q == 0:
            extra = jnp.where(whole, own_start, starts[...].reshape(nz, width))
        else:
            extra = jnp.where(whole, own_start, 0.0)
        value = rows_c[q, 0] + extra
        rows_y[q * nz : (q + 1) * nz] = value
        later = jnp.where(block_row < nz - 1, shifted(value, -1), 0.0)
        rows_y[(nx + q) * nz : (nx + q + 1) * nz] = later
    first = pl.multiple_of((1 + x) * nz, nz)
    tail = rows_y[pl.ds(first, nx * nz), :]
    for level in range(local_bits - 1, 2, -1):
        half = nz << (level - 3)
        tail = tail[:half] + times(tail[half:], gh[level], gl[level])
    for level in range(z_bits):
        distance = 1 << level
        moved = jnp.where(block_row < nz - distance, shifted(tail, -distance), 0.0)
        high, low = gh[local_bits + level], gl[local_bits + level]
        tail = tail + times(moved, high, low)
    after = jnp.sum(jnp.where(whole, tail, 0.0), axis=0, keepdims=True)

    row8 = lax.broadcasted_iota(jnp.int32, (steps, 1), 0)
    placed = jnp.where(row8 == steps - 1, after, 0.0)
    state = cbuf[x] + times(placed, gh[0], gl[0])
    for level in range(3):
        distance = 1 << level
        moved = jnp.where(row8 < steps - distance, shifted(state, -distance), 0.0)
        state = state + times(moved, gh[level], gl[level])
    copies_s = send_out(state, out_s, in_s, os_send, os_recv)

    odd = lax.rem(chan, 2) == 1
    half = BLOCK // 2
    for copies, into, result in ((copies_f, in_f, filtered), (copies_s, in_s, smoothed)):
        for copy in copies:
            copy.wait()
        both = into[...]
        result[...] = jnp.where(odd, both[:, :, half:], both[:, :, :half])


def build(mesh, nx):
    nc = mesh.shape["chan"]
    nz = mesh.shape["tm"] // nx

    def per_device(
        observations, obs_matrix, block_pattern, noise_precision, retention, prior_mean,
        filter_matrix, filter_gain, transition, smoother_gain,
    ):
        series, steps, channels = observations.shape
        width = obs_matrix.shape[1]
        span = nx * steps
        total = span * nz
        powers = total.bit_length() - 1
        vmem = pl.BlockSpec(memory_space=pltpu.VMEM)
        smem = pl.BlockSpec(memory_space=pltpu.SMEM)
        hbm = pl.BlockSpec(memory_space=pl.ANY)
        dma = pltpu.SemaphoreType.DMA
        square = (width, width)
        blocks = width // BLOCK
        result = jax.ShapeDtypeStruct((series, steps, width // nc), f32)
        return pl.pallas_call(
            functools.partial(kernel, nx, nz, nc, steps, width, channels),
            out_shape=(result, result),
            in_specs=[hbm, hbm, smem, vmem, vmem, vmem, hbm, hbm, hbm, hbm],
            out_specs=(vmem, vmem),
            scratch_shapes=[
                pltpu.VMEM((series, steps, channels), bf16),
                pltpu.VMEM((channels, width), bf16),
                pltpu.VMEM((4, *square), f32),
                pltpu.VMEM((powers, *square), bf16),
                pltpu.VMEM((powers, *square), bf16),
                pltpu.VMEM((powers, *square), bf16),
                pltpu.VMEM((powers, *square), bf16),
                pltpu.VMEM(square, bf16),
                pltpu.VMEM(square, bf16),
                pltpu.VMEM(square, bf16),
                pltpu.VMEM(square, bf16),
                pltpu.VMEM((nc, steps, width), f32),
                pltpu.VMEM((nc, steps, width), f32),
                pltpu.VMEM((nx, steps, width), f32),
                pltpu.VMEM((nz, 1, width), f32),
                pltpu.VMEM((nz, 1, width), f32),
                pltpu.VMEM((total, 1), f32),
                pltpu.VMEM((total, width), f32),
                pltpu.VMEM((nx, steps, nz, width), f32),
                pltpu.VMEM((nx, steps, width), f32),
                pltpu.VMEM((nx, steps, width), f32),
                pltpu.VMEM((nx, steps, width), f32),
                pltpu.VMEM((blocks, steps, BLOCK), f32),
                pltpu.VMEM((blocks, steps, BLOCK), f32),
                pltpu.VMEM((nc, steps, BLOCK), f32),
                pltpu.VMEM((nc, steps, BLOCK), f32),
                dma((6,)),
                dma((nc,)), dma((nc,)),
                dma((nx,)), dma((nx,)),
                dma((nz,)), dma((nz,)),
                dma((nz,)), dma((nz,)),
                dma((nc,)), dma((nc,)),
                dma((nc,)), dma((nc,)),
            ],
            compiler_params=pltpu.CompilerParams(
                collective_id=0, has_side_effects=True, vmem_limit_bytes=48 * 1024 * 1024
            ),
        )(
            observations, obs_matrix, block_pattern, noise_precision.reshape(1, channels),
            retention, prior_mean.reshape(1, width),
            filter_matrix, filter_gain, transition, smoother_gain,
        )

    placed = (
        P(None, "tm", "chan"), P("chan", None), P("chan", None), P("chan"),
        P(), P(), P(), P(), P(), P(),
    )
    return jax.shard_map(
        per_device,
        mesh=mesh,
        in_specs=placed,
        out_specs=(P(None, "tm", "chan"), P(None, "tm", "chan")),
        check_vma=False,
    )


def solution(mesh):
    return build(mesh, PLANE)
```

time: 1270 us -> 61.8 us (0.05)
  the two profiles are of different devices: /device:TPU:102 before, /device:TPU:1 now
where the time goes in v1:
time: 61.8 us; the launch traced here: 61.3 us
  Pallas kernels  49.9 us (81%)
  local copies, waits for them, and re-layouts  10.8 us (17%)
  between operations  0.66 us (1%)
    pallas_call x1, Pallas kernels, per_device(): pl.pallas_call(functools.partial(kernel, nx, nz, nc, steps, width, channe...  49.9 us
    unnamed x22, local copies, waits for them, and re-layouts  10.8 us

profile of v1, /device:TPU:1, one launch (start us, length us, event | category | flops | bytes accessed | tf_op | source)
XLA Modules:
  0.0 61.3 jit_solution(3184074778033927833)
XLA Ops:
  0.6 0.0 copy-start.7
  0.6 0.7 %copy-done.7 = s32[4,4]{1,0:T(4,128)S(1)} copy-done((s32[4,4]{1,0:T(4,128)S(1)}, s32[4,4]{1,0:T(4,128)}, u32[]{:S(2)}) %copy-start.7) | copy-done | bytes 88
  1.3 0.0 copy-start
  1.3 1.2 %copy-done = f32[512,512]{1,0:T(8,128)S(1)} copy-done((f32[512,512]{1,0:T(8,128)S(1)}, f32[512,512]{1,0:T(8,128)}, u32[]{:S(2)}) %copy-start) | copy-done | bytes 1048600
  2.5 0.0 copy-start.1
  2.5 1.2 %copy-done.1 = f32[512,512]{1,0:T(8,128)S(1)} copy-done((f32[512,512]{1,0:T(8,128)S(1)}, f32[512,512]{1,0:T(8,128)}, u32[]{:S(2)}) %copy-start.1) | copy-done | bytes 1048600
  3.8 0.0 copy-start.2
  3.8 1.2 %copy-done.2 = f32[512,512]{1,0:T(8,128)S(1)} copy-done((f32[512,512]{1,0:T(8,128)S(1)}, f32[512,512]{1,0:T(8,128)}, u32[]{:S(2)}) %copy-start.2) | copy-done | bytes 1048600
  5.0 0.0 copy-start.3
  5.0 1.2 %copy-done.3 = f32[512,512]{1,0:T(8,128)S(1)} copy-done((f32[512,512]{1,0:T(8,128)S(1)}, f32[512,512]{1,0:T(8,128)}, u32[]{:S(2)}) %copy-start.3) | copy-done | bytes 1048600
  6.2 0.0 copy-start.4
  6.2 1.0 %copy-done.4 = bf16[512,512]{1,0:T(8,128)(2,1)S(1)} copy-done((bf16[512,512]{1,0:T(8,128)(2,1)S(1)}, bf16[512,512]{1,0:T(8,128)(2,1)}, u32[]{:S(2)}) %copy-start.4) | copy-done | bytes 524312
  7.3 0.0 copy-start.5
  7.3 0.8 %copy-done.5 = bf16[8,8,512]{2,1,0:T(8,128)(2,1)S(1)} copy-done((bf16[8,8,512]{2,1,0:T(8,128)(2,1)S(1)}, bf16[8,8,512]{2,1,0:T(8,128)(2,1)}, u32[]{:S(2)}) %copy-start.5) | copy-done | bytes 65560
  8.1 0.0 copy-start.6
  8.1 0.7 %copy-done.6 = f32[8,512]{1,0:T(8,128)S(1)} copy-done((f32[8,512]{1,0:T(8,128)S(1)}, f32[8,512]{1,0:T(8,128)}, u32[]{:S(2)}) %copy-start.6) | copy-done | bytes 16408
  8.8 0.0 copy-start.8
  8.8 0.7 %copy-done.8 = f32[512]{0:T(512)S(1)} copy-done((f32[512]{0:T(512)S(1)}, f32[512]{0:T(512)}, u32[]{:S(2)}) %copy-start.8) | copy-done | bytes 2072
  9.5 0.0 copy-start.9
  9.5 0.7 %copy-done.9 = f32[512]{0:T(512)S(1)} copy-done((f32[512]{0:T(512)S(1)}, f32[512]{0:T(512)}, u32[]{:S(2)}) %copy-start.9) | copy-done | bytes 2072
  10.2 49.9 %shard_map.113 = (f32[8,8,64]{2,1,0:T(8,128)S(1)}, f32[8,8,64]{2,1,0:T(8,128)S(1)}) custom-call(bf16[8,8,512]{2,1,0:T(8,128)(2,1)S(1)} %copy-done.5, bf16[512,512]{1,0:T(8,128)(2,1)S(1)} %copy-done.4, s32[4,4]{1,0:T(4,128)S(1)} %copy-done.7, f32[1,512]{1,0:T(1,128)S(1)} %bitcast.2, f32[8,512]{1,0:T(8,128)S(1)} %copy-done.6, f32[1,512]{1,0:T(1,128)S(1)} %bitcast.3, ...), custom_call_target="tpu_custom_call" | custom-call | tf_op jit(solution)/shard_map/pallas_call | solution.py:339
  60.1 0.6 %copy.14 = f32[8,8,64]{2,1,0:T(8,128)} copy(f32[8,8,64]{2,1,0:T(8,128)S(1)} %get-tuple-element.4) | data formatting | bytes 32768
  60.7 0.6 %copy.15 = f32[8,8,64]{2,1,0:T(8,128)} copy(f32[8,8,64]{2,1,0:T(8,128)S(1)} %get-tuple-element.5) | data formatting | bytes 32768
Async XLA Ops:
  0.6 0.7 %copy-start.7 = (s32[4,4]{1,0:T(4,128)S(1)}, s32[4,4]{1,0:T(4,128)}, u32[]{:S(2)}) copy-start(s32[4,4]{1,0:T(4,128)} %pattern.1) | copy-start | bytes 196
  1.3 1.2 %copy-start = (f32[512,512]{1,0:T(8,128)S(1)}, f32[512,512]{1,0:T(8,128)}, u32[]{:S(2)}) copy-start(f32[512,512]{1,0:T(8,128)} %f_hbm.1) | copy-start | bytes 3145732
  2.5 1.2 %copy-start.1 = (f32[512,512]{1,0:T(8,128)S(1)}, f32[512,512]{1,0:T(8,128)}, u32[]{:S(2)}) copy-start(f32[512,512]{1,0:T(8,128)} %k_hbm.1) | copy-start | bytes 3145732
  3.8 1.2 %copy-start.2 = (f32[512,512]{1,0:T(8,128)S(1)}, f32[512,512]{1,0:T(8,128)}, u32[]{:S(2)}) copy-start(f32[512,512]{1,0:T(8,128)} %t_hbm.1) | copy-start | bytes 3145732
  5.0 1.2 %copy-start.3 = (f32[512,512]{1,0:T(8,128)S(1)}, f32[512,512]{1,0:T(8,128)}, u32[]{:S(2)}) copy-start(f32[512,512]{1,0:T(8,128)} %g_hbm.1) | copy-start | bytes 3145732
  6.2 1.0 %copy-start.4 = (bf16[512,512]{1,0:T(8,128)(2,1)S(1)}, bf16[512,512]{1,0:T(8,128)(2,1)}, u32[]{:S(2)}) copy-start(bf16[512,512]{1,0:T(8,128)(2,1)} %mat_hbm.1) | copy-start | bytes 1572868
  7.3 0.8 %copy-start.5 = (bf16[8,8,512]{2,1,0:T(8,128)(2,1)S(1)}, bf16[8,8,512]{2,1,0:T(8,128)(2,1)}, u32[]{:S(2)}) copy-start(bf16[8,8,512]{2,1,0:T(8,128)(2,1)} %obs_hbm.1) | copy-start | bytes 196612
  8.1 0.7 %copy-start.6 = (f32[8,512]{1,0:T(8,128)S(1)}, f32[8,512]{1,0:T(8,128)}, u32[]{:S(2)}) copy-start(f32[8,512]{1,0:T(8,128)} %retention.1) | copy-start | bytes 49156
  8.8 0.7 %copy-start.8 = (f32[512]{0:T(512)S(1)}, f32[512]{0:T(512)}, u32[]{:S(2)}) copy-start(f32[512]{0:T(512)} %param.13) | copy-start | bytes 6148
  9.5 0.7 %copy-start.9 = (f32[512]{0:T(512)S(1)}, f32[512]{0:T(512)}, u32[]{:S(2)}) copy-start(f32[512]{0:T(512)} %param.15) | copy-start | bytes 6148

commit v2 on v1

--- a/solution.py
+++ b/solution.py
@@ -9,6 +9,7 @@
 
 BLOCK = 128
 PLANE = 4
+LIMIT = 63 * 1024 * 1024
 MESH = pl.DeviceIdType.MESH
 f32 = jnp.float32
 bf16 = jnp.bfloat16
@@ -43,9 +44,9 @@
 
 def kernel(
     nx, nz, nc, steps, width, channels,
-    obs_hbm, mat_hbm, pattern, noise, retention, prior, f_hbm, k_hbm, t_hbm, g_hbm,
+    obs_hbm, mat_hbm, pattern_hbm, noise_hbm, retention_hbm, prior_hbm, f_hbm, k_hbm, t_hbm, g_hbm,
     filtered, smoothed,
-    obs, mat, raw, fh, fl, gh, gl, wh, wl, kh, kl,
+    obs, mat, pattern, noise, retention, prior, raw, fh, fl, gh, gl, wh, wl, kh, kl,
     part, part_in, drive, ends, starts, rho, rows_y, rows_c, fbuf, cbuf, bbuf,
     out_f, out_s, in_f, in_s,
     load_sem, rs_send, rs_recv, x_send, x_recv, e_send, e_recv, b_send, b_recv,
@@ -62,12 +63,16 @@
         pltpu.make_async_copy(source, target, load_sem.at[i])
         for i, (source, target) in enumerate(
             (
+                (obs_hbm, obs),
                 (mat_hbm, mat),
-                (obs_hbm, obs),
+                (pattern_hbm, pattern),
+                (noise_hbm, noise),
                 (f_hbm, raw.at[0]),
                 (k_hbm, raw.at[1]),
                 (g_hbm, raw.at[2]),
                 (t_hbm, raw.at[3]),
+                (retention_hbm, retention),
+                (prior_hbm, prior),
             )
         )
     ]
@@ -107,8 +112,8 @@
 
         lax.fori_loop(first, last, body, 0)
 
-    loads[0].wait()
-    loads[1].wait()
+    for load in loads[:4]:
+        load.wait()
     weighted = obs[...].astype(f32) * noise[...].reshape(1, 1, channels)
     weighted = weighted.reshape(nc * steps, channels).astype(bf16)
     lane_block = lax.broadcasted_iota(jnp.int32, (BLOCK, width), 1) // BLOCK
@@ -120,7 +125,7 @@
         used.append(mat[i * BLOCK : (i + 1) * BLOCK] * mask.astype(bf16))
     part[...] = dot(weighted, jnp.concatenate(used, 0)).reshape(nc, steps, width)
 
-    loads[2].wait()
+    loads[4].wait()
     fh[0], fl[0] = split(raw[0])
     square(fh, fl, 0, 2)
 
@@ -133,16 +138,24 @@
         sums.append(copy)
     part_in[chan] = part[chan]
 
+    loads[8].wait()
+    loads[9].wait()
     row = retention[pl.ds(chan, 1), :]
-    here = lax.broadcasted_iota(jnp.int32, (total, total), 0)
+    index = lax.broadcasted_iota(jnp.int32, (total, 1), 0)
+    plane, rest = index % nz, index // nz
+    wanted = plane * span + (rest % nx) * steps + rest // nx
     there = lax.broadcasted_iota(jnp.int32, (total, total), 1)
-    picked = jnp.where(there == (here % nz) * span + here // nz, row, 0.0)
-    column = jnp.sum(picked, axis=1, keepdims=True)
+    column = jnp.sum(jnp.where(there == wanted, row, 0.0), axis=1, keepdims=True)
+
+    def rows_of(t):
+        start = ((t % steps) * nx + t // steps) * nz
+        return slice(start, start + nz)
+
     running = column[:nz]
     rho[:nz] = running
     for t in range(1, span):
-        running = running * column[t * nz : (t + 1) * nz]
-        rho[t * nz : (t + 1) * nz] = running
+        running = running * column[rows_of(t)]
+        rho[rows_of(t)] = running
     block_row = lax.broadcasted_iota(jnp.int32, (nz, 1), 0)
     chain = jnp.where(block_row >= 1, shifted(running, 1), 0.0)
     block_factors = [chain]
@@ -158,9 +171,19 @@
         own = own * shifted(own, 1 << (level - 1))
         own_factors.append(jnp.where(step_row >= (1 << level), own, 0.0))
 
-    loads[3].wait()
+    loads[5].wait()
     kh[...], kl[...] = split(raw[1])
-    square(fh, fl, 2, local_bits)
+    square(fh, fl, 2, 4)
+
+    loads[6].wait()
+    loads[7].wait()
+    gh[0], gl[0] = split(raw[2])
+    th, tl = split(raw[3])
+    eye = lax.broadcasted_iota(jnp.int32, (width, width), 0) == lax.broadcasted_iota(
+        jnp.int32, (width, width), 1
+    )
+    product = dot(th, gh[0]) + (dot(th, gl[0]) + dot(tl, gh[0]))
+    wh[...], wl[...] = split(jnp.where(eye, 1.0, 0.0) - product)
 
     for copy in sums:
         copy.wait()
@@ -174,15 +197,6 @@
         copy.start()
         spread.append(copy)
 
-    loads[4].wait()
-    loads[5].wait()
-    gh[0], gl[0] = split(raw[2])
-    th, tl = split(raw[3])
-    eye = lax.broadcasted_iota(jnp.int32, (width, width), 0) == lax.broadcasted_iota(
-        jnp.int32, (width, width), 1
-    )
-    product = dot(th, gh[0]) + (dot(th, gl[0]) + dot(tl, gh[0]))
-    wh[...], wl[...] = split(jnp.where(eye, 1.0, 0.0) - product)
     square(gh, gl, 0, 3)
 
     for copy in spread:
@@ -193,6 +207,7 @@
         moved = shifted(local, 1 << level)
         local = local + own_factors[level] * times(moved, fh[level], fl[level])
     ends[z] = local[span - 1 :]
+    fbuf[...] = local.reshape(nx, steps, width)
     across = []
     for i in sorted(range(1, nz), key=lambda i: -min(i, nz - i)):
         copy = remote(ends.at[z], ends.at[z], e_send.at[i], e_recv.at[i], z_peer(i))
@@ -203,6 +218,7 @@
     last_plane = z == nz - 1
     corrected = times(local, wh[...], wl[...])
     corrected = jnp.where(last_plane & (step_row == span - 1), local, corrected)
+    cbuf[...] = corrected.reshape(nx, steps, width)
     backward = corrected
     for level in (2, 1, 0):
         backward = backward + times(shifted(backward, -(1 << level)), gh[level], gl[level])
@@ -215,7 +231,7 @@
         copy.start()
         across.append(copy)
 
-    square(fh, fl, local_bits, local_bits + z_bits - 1)
+    square(fh, fl, 4, local_bits + z_bits - 1)
     square(gh, gl, 4, local_bits + z_bits - 1)
 
     for copy in across[: nz - 1]:
@@ -228,13 +244,14 @@
         carry = carry + block_factors[level] * times(moved, high, low)
 
     rows_y[:nz] = times(carry, fh[0], fl[0])
-    for level in range(local_bits):
-        count = nz << level
+    count = nz
+    for level in (*range(3, local_bits), 0, 1, 2):
         rows_y[count : 2 * count] = times(rows_y[:count], fh[level], fl[level])
-    scaled = rows_y[...] * rho[...]
-    is_own = lax.broadcasted_iota(jnp.int32, (1, nz, 1), 1) == z
-    picked = jnp.sum(jnp.where(is_own, scaled.reshape(span, nz, width), 0.0), axis=1)
-    fbuf[...] = (local + picked).reshape(nx, steps, width)
+        count = 2 * count
+    rows_y[...] = rows_y[...] * rho[...]
+
+    def own_rows(rows):
+        return jnp.concatenate([rows[pl.ds((p * nx + x) * nz + z, 1), :] for p in range(steps)], 0)
 
     def send_out(state, out, into, send, recv):
         copies = []
@@ -248,30 +265,15 @@
         into[chan] = out[chan // 2]
         return copies
 
-    copies_f = send_out(fbuf[x], out_f, in_f, of_send, of_recv)
-
-    turned = times(rows_y[...] * rho[...], wh[...], wl[...])
-    final = lax.broadcasted_iota(jnp.int32, (total, 1), 0) == total - 1
-    turned = jnp.where(final, rows_y[...] * rho[...], turned)
-    rows_c[...] = turned.reshape(nx, steps, nz, width)
-    for t in range(span):
-        row = rows_c[t // steps, t % steps]
-        row = jnp.sum(jnp.where(block_row == z, row, 0.0), axis=0, keepdims=True)
-        cbuf[t // steps, t % steps : t % steps + 1] = row
-    cbuf[...] = cbuf[...] + corrected.reshape(nx, steps, width)
+    copies_f = send_out(fbuf[x] + own_rows(rows_y), out_f, in_f, of_send, of_recv)
+
+    rows_c[...] = times(rows_y[...], wh[...], wl[...])
+    rows_c[total - 1 :] = rows_y[total - 1 :]
+    own_corrected = cbuf[x] + own_rows(rows_c)
 
     for level in (2, 1, 0):
-        half = 1 << level
-        few = max(1, min(nx, 128 // (half * nz)))
-
-        def reduce_rows(i, _):
-            q = pl.ds(i * few, few)
-            upper = rows_c[q, half : 2 * half].reshape(few * half * nz, width)
-            upper = times(upper, gh[level], gl[level]).reshape(few, half, nz, width)
-            rows_c[q, :half] = rows_c[q, :half] + upper
-            return 0
-
-        lax.fori_loop(0, nx // few, reduce_rows, 0)
+        half = nx * nz << level
+        rows_c[:half] = rows_c[:half] + times(rows_c[half : 2 * half], gh[level], gl[level])
 
     for copy in across[nz - 1 :]:
         copy.wait()
@@ -282,7 +284,7 @@
             extra = jnp.where(whole, own_start, starts[...].reshape(nz, width))
         else:
             extra = jnp.where(whole, own_start, 0.0)
-        value = rows_c[q, 0] + extra
+        value = rows_c[q * nz : (q + 1) * nz] + extra
         rows_y[q * nz : (q + 1) * nz] = value
         later = jnp.where(block_row < nz - 1, shifted(value, -1), 0.0)
         rows_y[(nx + q) * nz : (nx + q + 1) * nz] = later
@@ -300,20 +302,17 @@
 
     row8 = lax.broadcasted_iota(jnp.int32, (steps, 1), 0)
     placed = jnp.where(row8 == steps - 1, after, 0.0)
-    state = cbuf[x] + times(placed, gh[0], gl[0])
+    state = own_corrected + times(placed, gh[0], gl[0])
     for level in range(3):
         distance = 1 << level
         moved = jnp.where(row8 < steps - distance, shifted(state, -distance), 0.0)
         state = state + times(moved, gh[level], gl[level])
     copies_s = send_out(state, out_s, in_s, os_send, os_recv)
 
-    odd = lax.rem(chan, 2) == 1
-    half = BLOCK // 2
     for copies, into, result in ((copies_f, in_f, filtered), (copies_s, in_s, smoothed)):
         for copy in copies:
             copy.wait()
-        both = into[...]
-        result[...] = jnp.where(odd, both[:, :, half:], both[:, :, :half])
+        result[...] = into[...]
 
 
 def build(mesh, nx):
@@ -330,20 +329,23 @@
         total = span * nz
         powers = total.bit_length() - 1
         vmem = pl.BlockSpec(memory_space=pltpu.VMEM)
-        smem = pl.BlockSpec(memory_space=pltpu.SMEM)
         hbm = pl.BlockSpec(memory_space=pl.ANY)
         dma = pltpu.SemaphoreType.DMA
         square = (width, width)
         blocks = width // BLOCK
-        result = jax.ShapeDtypeStruct((series, steps, width // nc), f32)
-        return pl.pallas_call(
+        result = jax.ShapeDtypeStruct((series, steps, BLOCK), f32)
+        both = pl.pallas_call(
             functools.partial(kernel, nx, nz, nc, steps, width, channels),
             out_shape=(result, result),
-            in_specs=[hbm, hbm, smem, vmem, vmem, vmem, hbm, hbm, hbm, hbm],
+            in_specs=[hbm] * 10,
             out_specs=(vmem, vmem),
             scratch_shapes=[
                 pltpu.VMEM((series, steps, channels), bf16),
                 pltpu.VMEM((channels, width), bf16),
+                pltpu.SMEM((channels // BLOCK, width // BLOCK), jnp.int32),
+                pltpu.VMEM((1, channels), f32),
+                pltpu.VMEM((series, total), f32),
+                pltpu.VMEM((1, width), f32),
                 pltpu.VMEM((4, *square), f32),
                 pltpu.VMEM((powers, *square), bf16),
                 pltpu.VMEM((powers, *square), bf16),
@@ -360,7 +362,7 @@
                 pltpu.VMEM((nz, 1, width), f32),
                 pltpu.VMEM((total, 1), f32),
                 pltpu.VMEM((total, width), f32),
-                pltpu.VMEM((nx, steps, nz, width), f32),
+                pltpu.VMEM((total, width), f32),
                 pltpu.VMEM((nx, steps, width), f32),
                 pltpu.VMEM((nx, steps, width), f32),
                 pltpu.VMEM((nx, steps, width), f32),
@@ -368,7 +370,7 @@
                 pltpu.VMEM((blocks, steps, BLOCK), f32),
                 pltpu.VMEM((nc, steps, BLOCK), f32),
                 pltpu.VMEM((nc, steps, BLOCK), f32),
-                dma((6,)),
+                dma((10,)),
                 dma((nc,)), dma((nc,)),
                 dma((nx,)), dma((nx,)),
                 dma((nz,)), dma((nz,)),
@@ -377,13 +379,16 @@
                 dma((nc,)), dma((nc,)),
             ],
             compiler_params=pltpu.CompilerParams(
-                collective_id=0, has_side_effects=True, vmem_limit_bytes=48 * 1024 * 1024
+                collective_id=0, has_side_effects=True, vmem_limit_bytes=LIMIT
             ),
         )(
             observations, obs_matrix, block_pattern, noise_precision.reshape(1, channels),
             retention, prior_mean.reshape(1, width),
             filter_matrix, filter_gain, transition, smoother_gain,
         )
+        odd = lax.rem(lax.axis_index("chan"), 2) == 1
+        half = BLOCK // 2
+        return tuple(jnp.where(odd, array[:, :, half:], array[:, :, :half]) for array in both)
 
     placed = (
         P(None, "tm", "chan"), P("chan", None), P("chan", None), P("chan"),

time: 61.8 us -> 52.5 us (0.85)
  local copies, waits for them, and re-layouts: 10.8 us -> 0 us
  other arithmetic: 0 us -> 1.56 us
    unnamed x22 -> x0, local copies, waits for them, and re-layouts: 10.8 us -> none
    select_n x0 -> x1, other arithmetic: none -> 1.56 us  [per_device(): jnp.where(odd, array[:, :, half:], array[:, :, :half])]
where the time goes in v2:
time: 52.5 us; the launch traced here: 52.3 us
  Pallas kernels  50.1 us (95%)
  other arithmetic  1.56 us (3%)
  between operations  0.65 us (1%)
    pallas_call x1, Pallas kernels, per_device(): pl.pallas_call(functools.partial(kernel, nx, nz, nc, steps, width, channe...  50.1 us
    select_n x1, other arithmetic, per_device(): jnp.where(odd, array[:, :, half:], array[:, :, :half])  1.56 us

profile of v2, /device:TPU:1, one launch (start us, length us, event | category | flops | bytes accessed | tf_op | source)
XLA Modules:
  0.0 52.3 jit_solution(14644900450873874936)
XLA Ops:
  0.6 50.1 %shard_map.113 = (f32[8,8,128]{2,1,0:T(8,128)}, f32[8,8,128]{2,1,0:T(8,128)}) custom-call(bf16[8,8,512]{2,1,0:T(8,128)(2,1)} %obs_hbm.1, bf16[512,512]{1,0:T(8,128)(2,1)} %mat_hbm.1, s32[4,4]{1,0:T(4,128)} %pattern_hbm.1, f32[1,512]{1,0:T(1,128)} %bitcast.2, f32[8,512]{1,0:T(8,128)} %retention_hbm.1, f32[1,512]{1,0:T(1,128)} %bitcast.3, f32[512,512]{1,0:T(8,128)} %f_hbm.1, ...), custom_call_target="tpu_custom_call" | custom-call | tf_op jit(solution)/shard_map/pallas_call | solution.py:337
  50.8 1.6 %slice_select_fusion = (f32[8,8,64]{2,1,0:T(8,128)}, f32[8,8,64]{2,1,0:T(8,128)}) fusion(f32[8,8,128]{2,1,0:T(8,128)} %get-tuple-element.5, pred[]{:T(512)S(6)} %eq.3, f32[8,8,128]{2,1,0:T(8,128)} %get-tuple-element.4), kind=kLoop, calls=%fused_computation | loop fusion | flops 8192 | bytes 98305 | tf_op jit(solution)/shard_map/jit(_where)/select_n | solution.py:391

commit v3 on v2

--- a/solution.py
+++ b/solution.py
@@ -9,6 +9,7 @@
 
 BLOCK = 128
 PLANE = 4
+NEAR = 2
 LIMIT = 63 * 1024 * 1024
 MESH = pl.DeviceIdType.MESH
 f32 = jnp.float32
@@ -46,11 +47,11 @@
     nx, nz, nc, steps, width, channels,
     obs_hbm, mat_hbm, pattern_hbm, noise_hbm, retention_hbm, prior_hbm, f_hbm, k_hbm, t_hbm, g_hbm,
     filtered, smoothed,
-    obs, mat, pattern, noise, retention, prior, raw, fh, fl, gh, gl, wh, wl, kh, kl,
-    part, part_in, drive, ends, starts, rho, rows_y, rows_c, fbuf, cbuf, bbuf,
+    obs, mat, pattern, noise, retention, prior, raw, fgh, fgl, wh, wl, kh, kl,
+    own_power, other_power, part, part_in, drive, ends, starts, rho, rows_y, rows_c, fbuf, cbuf, bbuf,
     out_f, out_s, in_f, in_s,
     load_sem, rs_send, rs_recv, x_send, x_recv, e_send, e_recv, b_send, b_recv,
-    of_send, of_recv, os_send, os_recv,
+    of_send, of_recv, os_send, os_recv, pow_send, pow_recv, ready,
 ):
     tm, chan = lax.axis_index("tm"), lax.axis_index("chan")
     z, x = tm // nx, tm % nx
@@ -88,26 +89,62 @@
     def z_peer(i):
         return {"tm": lax.rem(z + i, nz) * nx + x}
 
+    near = [i for i in range(1, nz) if min(i, nz - i) <= NEAR]
     barrier = pltpu.get_barrier_semaphore()
-    for i in range(1, nz):
+    for i in near:
         pl.semaphore_signal(barrier, inc=1, device_id=z_peer(i), device_id_type=MESH)
     for i in range(1, nx):
         pl.semaphore_signal(barrier, inc=1, device_id=x_peer(i), device_id_type=MESH)
     for i in range(1, nc):
         pl.semaphore_signal(barrier, inc=1, device_id=chan_peer(i), device_id_type=MESH)
 
+    def ring(distance):
+        return sorted({i for i in (distance, nz - distance) if 0 < i < nz})
+
+    rounds = [d for d in (NEAR, 2 * NEAR) if 2 * d <= nz // 2]
+
+    def widen(k):
+        for i in ring(rounds[k]):
+            pl.semaphore_signal(ready.at[k], inc=1, device_id=z_peer(i), device_id_type=MESH)
+
+    def widened(k):
+        pl.semaphore_wait(ready.at[k], len(ring(rounds[k])))
+
     def remote(source, target, send, recv, peer):
         return pltpu.make_async_remote_copy(
             src_ref=source, dst_ref=target, send_sem=send, recv_sem=recv,
             device_id=peer, device_id_type=MESH,
         )
 
-    def square(high, low, first, last):
+    fh, fl, gh, gl = fgh.at[0], fgl.at[0], fgh.at[1], fgl.at[1]
+    core = lax.rem(chan, 2)
+    twin = {"chan": chan + 1 - 2 * core}
+
+    def power_copy(i):
+        return remote(own_power.at[i], other_power.at[i], pow_send.at[i], pow_recv.at[i], twin)
+
+    def square(first, last):
         def body(i, _):
-            a, b = high[i], low[i]
-            h, l = split(dot(a, a) + (dot(a, b) + dot(b, a)))
-            high[i + 1] = h
-            low[i + 1] = l
+            a, b = fgh[core, i], fgl[core, i]
+            product = dot(a, a) + (dot(a, b) + dot(b, a))
+            own_power[i] = product
+            h, l = split(product)
+            fgh[core, i + 1] = h
+            fgl[core, i + 1] = l
+            return 0
+
+        lax.fori_loop(first, last, body, 0)
+
+    def send_powers(first, last):
+        for i in range(first, last):
+            power_copy(i).start()
+
+    def take_powers(first, last):
+        def body(i, _):
+            power_copy(i).wait_recv()
+            h, l = split(other_power[i])
+            fgh[1 - core, i + 1] = h
+            fgl[1 - core, i + 1] = l
             return 0
 
         lax.fori_loop(first, last, body, 0)
@@ -126,10 +163,12 @@
     part[...] = dot(weighted, jnp.concatenate(used, 0)).reshape(nc, steps, width)
 
     loads[4].wait()
-    fh[0], fl[0] = split(raw[0])
-    square(fh, fl, 0, 2)
-
-    pl.semaphore_wait(barrier, nz + nx + nc - 3)
+    loads[6].wait()
+    for which in range(2):
+        fgh[which, 0], fgl[which, 0] = split(raw[2 * which])
+    square(0, 2)
+
+    pl.semaphore_wait(barrier, len(near) + nx + nc - 2)
     sums = []
     for i in range(1, nc):
         there = lax.rem(chan + i, nc)
@@ -137,6 +176,9 @@
         copy.start()
         sums.append(copy)
     part_in[chan] = part[chan]
+    send_powers(0, 2)
+    if rounds:
+        widen(0)
 
     loads[8].wait()
     loads[9].wait()
@@ -173,11 +215,12 @@
 
     loads[5].wait()
     kh[...], kl[...] = split(raw[1])
-    square(fh, fl, 2, 4)
-
-    loads[6].wait()
+    square(2, 4)
+    send_powers(2, 4)
+    square(4, 5)
+    send_powers(4, 5)
+
     loads[7].wait()
-    gh[0], gl[0] = split(raw[2])
     th, tl = split(raw[3])
     eye = lax.broadcasted_iota(jnp.int32, (width, width), 0) == lax.broadcasted_iota(
         jnp.int32, (width, width), 1
@@ -187,6 +230,10 @@
 
     for copy in sums:
         copy.wait()
+    if rounds:
+        widened(0)
+    if len(rounds) > 1:
+        widen(1)
     information = part_in[0]
     for i in range(1, nc):
         information = information + part_in[i]
@@ -197,10 +244,14 @@
         copy.start()
         spread.append(copy)
 
-    square(gh, gl, 0, 3)
+    square(5, local_bits + z_bits - 1)
+    send_powers(5, local_bits + z_bits - 1)
+    take_powers(0, 4)
 
     for copy in spread:
         copy.wait()
+    if len(rounds) > 1:
+        widened(1)
 
     local = drive[...].reshape(span, width)
     for level in range(local_bits):
@@ -214,7 +265,6 @@
         copy.start()
         across.append(copy)
 
-    square(gh, gl, 3, 4)
     last_plane = z == nz - 1
     corrected = times(local, wh[...], wl[...])
     corrected = jnp.where(last_plane & (step_row == span - 1), local, corrected)
@@ -231,8 +281,7 @@
         copy.start()
         across.append(copy)
 
-    square(fh, fl, 4, local_bits + z_bits - 1)
-    square(gh, gl, 4, local_bits + z_bits - 1)
+    take_powers(4, local_bits + z_bits - 1)
 
     for copy in across[: nz - 1]:
         copy.wait()
@@ -309,6 +358,8 @@
         state = state + times(moved, gh[level], gl[level])
     copies_s = send_out(state, out_s, in_s, os_send, os_recv)
 
+    for i in range(local_bits + z_bits - 1):
+        power_copy(i).wait_send()
     for copies, into, result in ((copies_f, in_f, filtered), (copies_s, in_s, smoothed)):
         for copy in copies:
             copy.wait()
@@ -347,14 +398,14 @@
                 pltpu.VMEM((series, total), f32),
                 pltpu.VMEM((1, width), f32),
                 pltpu.VMEM((4, *square), f32),
-                pltpu.VMEM((powers, *square), bf16),
-                pltpu.VMEM((powers, *square), bf16),
-                pltpu.VMEM((powers, *square), bf16),
-                pltpu.VMEM((powers, *square), bf16),
+                pltpu.VMEM((2, powers, *square), bf16),
+                pltpu.VMEM((2, powers, *square), bf16),
                 pltpu.VMEM(square, bf16),
                 pltpu.VMEM(square, bf16),
                 pltpu.VMEM(square, bf16),
                 pltpu.VMEM(square, bf16),
+                pltpu.VMEM((powers - 1, *square), f32),
+                pltpu.VMEM((powers - 1, *square), f32),
                 pltpu.VMEM((nc, steps, width), f32),
                 pltpu.VMEM((nc, steps, width), f32),
                 pltpu.VMEM((nx, steps, width), f32),
@@ -377,6 +428,8 @@
                 dma((nz,)), dma((nz,)),
                 dma((nc,)), dma((nc,)),
                 dma((nc,)), dma((nc,)),
+                dma((powers,)), dma((powers,)),
+                pltpu.SemaphoreType.REGULAR((2,)),
             ],
             compiler_params=pltpu.CompilerParams(
                 collective_id=0, has_side_effects=True, vmem_limit_bytes=LIMIT

time: 52.5 us -> 49.2 us (0.937)
  Pallas kernels: 50.1 us -> 46.8 us
    pallas_call x1, Pallas kernels: 50.1 us -> 46.8 us  [per_device(): pl.pallas_call(functools.partial(kernel, nx, nz, nc, steps, width, channe...]
where the time goes in v3:
time: 49.2 us; the launch traced here: 49 us
  Pallas kernels  46.8 us (95%)
  other arithmetic  1.56 us (3%)
  between operations  0.65 us (1%)
    pallas_call x1, Pallas kernels, per_device(): pl.pallas_call(functools.partial(kernel, nx, nz, nc, steps, width, channe...  46.8 us
    select_n x1, other arithmetic, per_device(): jnp.where(odd, array[:, :, half:], array[:, :, :half])  1.56 us

profile of v3, /device:TPU:1, one launch (start us, length us, event | category | flops | bytes accessed | tf_op | source)
XLA Modules:
  0.0 49.0 jit_solution(3889085824563194047)
XLA Ops:
  0.6 46.8 %shard_map.113 = (f32[8,8,128]{2,1,0:T(8,128)}, f32[8,8,128]{2,1,0:T(8,128)}) custom-call(bf16[8,8,512]{2,1,0:T(8,128)(2,1)} %obs_hbm.1, bf16[512,512]{1,0:T(8,128)(2,1)} %mat_hbm.1, s32[4,4]{1,0:T(4,128)} %pattern_hbm.1, f32[1,512]{1,0:T(1,128)} %bitcast.2, f32[8,512]{1,0:T(8,128)} %retention_hbm.1, f32[1,512]{1,0:T(1,128)} %bitcast.3, f32[512,512]{1,0:T(8,128)} %f_hbm.1, ...), custom_call_target="tpu_custom_call" | custom-call | tf_op jit(solution)/shard_map/pallas_call | solution.py:388
  47.4 1.6 %slice_select_fusion = (f32[8,8,64]{2,1,0:T(8,128)}, f32[8,8,64]{2,1,0:T(8,128)}) fusion(f32[8,8,128]{2,1,0:T(8,128)} %get-tuple-element.5, pred[]{:T(512)S(6)} %eq.3, f32[8,8,128]{2,1,0:T(8,128)} %get-tuple-element.4), kind=kLoop, calls=%fused_computation | loop fusion | flops 8192 | bytes 98305 | tf_op jit(solution)/shard_map/jit(_where)/select_n | solution.py:444

commit v4 on v3

--- a/solution.py
+++ b/solution.py
@@ -123,11 +123,13 @@
     def power_copy(i):
         return remote(own_power.at[i], other_power.at[i], pow_send.at[i], pow_recv.at[i], twin)
 
-    def square(first, last):
+    def square(first, last, send=True):
         def body(i, _):
             a, b = fgh[core, i], fgl[core, i]
             product = dot(a, a) + (dot(a, b) + dot(b, a))
             own_power[i] = product
+            if send:
+                power_copy(i).start()
             h, l = split(product)
             fgh[core, i + 1] = h
             fgl[core, i + 1] = l
@@ -164,9 +166,8 @@
 
     loads[4].wait()
     loads[6].wait()
-    for which in range(2):
-        fgh[which, 0], fgl[which, 0] = split(raw[2 * which])
-    square(0, 2)
+    fgh[core, 0], fgl[core, 0] = split(raw[2 * core])
+    square(0, 1, send=False)
 
     pl.semaphore_wait(barrier, len(near) + nx + nc - 2)
     sums = []
@@ -176,9 +177,11 @@
         copy.start()
         sums.append(copy)
     part_in[chan] = part[chan]
-    send_powers(0, 2)
+    send_powers(0, 1)
     if rounds:
         widen(0)
+    square(1, 4)
+    fgh[1 - core, 0], fgl[1 - core, 0] = split(raw[2 * (1 - core)])
 
     loads[8].wait()
     loads[9].wait()
@@ -215,25 +218,10 @@
 
     loads[5].wait()
     kh[...], kl[...] = split(raw[1])
-    square(2, 4)
-    send_powers(2, 4)
-    square(4, 5)
-    send_powers(4, 5)
-
-    loads[7].wait()
-    th, tl = split(raw[3])
-    eye = lax.broadcasted_iota(jnp.int32, (width, width), 0) == lax.broadcasted_iota(
-        jnp.int32, (width, width), 1
-    )
-    product = dot(th, gh[0]) + (dot(th, gl[0]) + dot(tl, gh[0]))
-    wh[...], wl[...] = split(jnp.where(eye, 1.0, 0.0) - product)
+
 
     for copy in sums:
         copy.wait()
-    if rounds:
-        widened(0)
-    if len(rounds) > 1:
-        widen(1)
     information = part_in[0]
     for i in range(1, nc):
         information = information + part_in[i]
@@ -244,9 +232,19 @@
         copy.start()
         spread.append(copy)
 
-    square(5, local_bits + z_bits - 1)
-    send_powers(5, local_bits + z_bits - 1)
+    if rounds:
+        widened(0)
+    if len(rounds) > 1:
+        widen(1)
+    loads[7].wait()
+    th, tl = split(raw[3])
+    eye = lax.broadcasted_iota(jnp.int32, (width, width), 0) == lax.broadcasted_iota(
+        jnp.int32, (width, width), 1
+    )
+    product = dot(th, gh[0]) + (dot(th, gl[0]) + dot(tl, gh[0]))
+    wh[...], wl[...] = split(jnp.where(eye, 1.0, 0.0) - product)
     take_powers(0, 4)
+    square(4, 5)
 
     for copy in spread:
         copy.wait()
@@ -264,6 +262,8 @@
         copy = remote(ends.at[z], ends.at[z], e_send.at[i], e_recv.at[i], z_peer(i))
         copy.start()
         across.append(copy)
+
+    square(5, local_bits + z_bits - 1)
 
     last_plane = z == nz - 1
     corrected = times(local, wh[...], wl[...])

time: 49.2 us -> 47.7 us (0.970)
  Pallas kernels: 46.8 us -> 45.3 us
    pallas_call x1, Pallas kernels: 46.8 us -> 45.3 us  [per_device(): pl.pallas_call(functools.partial(kernel, nx, nz, nc, steps, width, channe...]
where the time goes in v4:
time: 47.7 us; the launch traced here: 47.5 us
  Pallas kernels  45.3 us (95%)
  other arithmetic  1.56 us (3%)
  between operations  0.65 us (1%)
    pallas_call x1, Pallas kernels, per_device(): pl.pallas_call(functools.partial(kernel, nx, nz, nc, steps, width, channe...  45.3 us
    select_n x1, other arithmetic, per_device(): jnp.where(odd, array[:, :, half:], array[:, :, :half])  1.56 us

profile of v4, /device:TPU:1, one launch (start us, length us, event | category | flops | bytes accessed | tf_op | source)
XLA Modules:
  0.0 47.5 jit_solution(5445428850661314736)
XLA Ops:
  0.6 45.3 %shard_map.113 = (f32[8,8,128]{2,1,0:T(8,128)}, f32[8,8,128]{2,1,0:T(8,128)}) custom-call(bf16[8,8,512]{2,1,0:T(8,128)(2,1)} %obs_hbm.1, bf16[512,512]{1,0:T(8,128)(2,1)} %mat_hbm.1, s32[4,4]{1,0:T(4,128)} %pattern_hbm.1, f32[1,512]{1,0:T(1,128)} %bitcast.2, f32[8,512]{1,0:T(8,128)} %retention_hbm.1, f32[1,512]{1,0:T(1,128)} %bitcast.3, f32[512,512]{1,0:T(8,128)} %f_hbm.1, ...), custom_call_target="tpu_custom_call" | custom-call | tf_op jit(solution)/shard_map/pallas_call | solution.py:388
  45.9 1.6 %slice_select_fusion = (f32[8,8,64]{2,1,0:T(8,128)}, f32[8,8,64]{2,1,0:T(8,128)}) fusion(f32[8,8,128]{2,1,0:T(8,128)} %get-tuple-element.5, pred[]{:T(512)S(6)} %eq.3, f32[8,8,128]{2,1,0:T(8,128)} %get-tuple-element.4), kind=kLoop, calls=%fused_computation | loop fusion | flops 8192 | bytes 98305 | tf_op jit(solution)/shard_map/jit(_where)/select_n | solution.py:444

commit v5 on v4

--- a/solution.py
+++ b/solution.py
@@ -47,7 +47,7 @@
     nx, nz, nc, steps, width, channels,
     obs_hbm, mat_hbm, pattern_hbm, noise_hbm, retention_hbm, prior_hbm, f_hbm, k_hbm, t_hbm, g_hbm,
     filtered, smoothed,
-    obs, mat, pattern, noise, retention, prior, raw, fgh, fgl, wh, wl, kh, kl,
+    obs, mat, pattern, noise, retention, prior, raw, fgh, fgl, wh, wl,
     own_power, other_power, part, part_in, drive, ends, starts, rho, rows_y, rows_c, fbuf, cbuf, bbuf,
     out_f, out_s, in_f, in_s,
     load_sem, rs_send, rs_recv, x_send, x_recv, e_send, e_recv, b_send, b_recv,
@@ -68,8 +68,8 @@
                 (mat_hbm, mat),
                 (pattern_hbm, pattern),
                 (noise_hbm, noise),
+                (k_hbm, raw.at[1]),
                 (f_hbm, raw.at[0]),
-                (k_hbm, raw.at[1]),
                 (g_hbm, raw.at[2]),
                 (t_hbm, raw.at[3]),
                 (retention_hbm, retention),
@@ -91,12 +91,13 @@
 
     near = [i for i in range(1, nz) if min(i, nz - i) <= NEAR]
     barrier = pltpu.get_barrier_semaphore()
+    for i in range(1, nc):
+        pl.semaphore_signal(barrier, inc=1, device_id=chan_peer(i), device_id_type=MESH)
+
+    for i in range(1, nx):
+        pl.semaphore_signal(barrier, inc=1, device_id=x_peer(i), device_id_type=MESH)
     for i in near:
         pl.semaphore_signal(barrier, inc=1, device_id=z_peer(i), device_id_type=MESH)
-    for i in range(1, nx):
-        pl.semaphore_signal(barrier, inc=1, device_id=x_peer(i), device_id_type=MESH)
-    for i in range(1, nc):
-        pl.semaphore_signal(barrier, inc=1, device_id=chan_peer(i), device_id_type=MESH)
 
     def ring(distance):
         return sorted({i for i in (distance, nz - distance) if 0 < i < nz})
@@ -109,6 +110,9 @@
 
     def widened(k):
         pl.semaphore_wait(ready.at[k], len(ring(rounds[k])))
+
+    def far_first(count):
+        return sorted(range(1, count), key=lambda i: -min(i, count - i))
 
     def remote(source, target, send, recv, peer):
         return pltpu.make_async_remote_copy(
@@ -123,23 +127,18 @@
     def power_copy(i):
         return remote(own_power.at[i], other_power.at[i], pow_send.at[i], pow_recv.at[i], twin)
 
-    def square(first, last, send=True):
+    def square(first, last):
         def body(i, _):
             a, b = fgh[core, i], fgl[core, i]
             product = dot(a, a) + (dot(a, b) + dot(b, a))
             own_power[i] = product
-            if send:
-                power_copy(i).start()
+            power_copy(i).start()
             h, l = split(product)
             fgh[core, i + 1] = h
             fgl[core, i + 1] = l
             return 0
 
         lax.fori_loop(first, last, body, 0)
-
-    def send_powers(first, last):
-        for i in range(first, last):
-            power_copy(i).start()
 
     def take_powers(first, last):
         def body(i, _):
@@ -162,26 +161,27 @@
         for j in range(width // BLOCK):
             mask = jnp.where(lane_block == j, pattern[i, j].astype(f32), mask)
         used.append(mat[i * BLOCK : (i + 1) * BLOCK] * mask.astype(bf16))
-    part[...] = dot(weighted, jnp.concatenate(used, 0)).reshape(nc, steps, width)
+    information = dot(weighted, jnp.concatenate(used, 0))
 
     loads[4].wait()
-    loads[6].wait()
-    fgh[core, 0], fgl[core, 0] = split(raw[2 * core])
-    square(0, 1, send=False)
+    kh, kl = split(raw[1])
+    part[...] = times(information, kh, kl).reshape(nc, steps, width)
+
 
     pl.semaphore_wait(barrier, len(near) + nx + nc - 2)
     sums = []
-    for i in range(1, nc):
+    for i in far_first(nc):
         there = lax.rem(chan + i, nc)
         copy = remote(part.at[there], part_in.at[chan], rs_send.at[i], rs_recv.at[i], chan_peer(i))
         copy.start()
         sums.append(copy)
     part_in[chan] = part[chan]
-    send_powers(0, 1)
     if rounds:
         widen(0)
-    square(1, 4)
-    fgh[1 - core, 0], fgl[1 - core, 0] = split(raw[2 * (1 - core)])
+    loads[5].wait()
+    loads[6].wait()
+    fgh[core, 0], fgl[core, 0] = split(raw[2 * core])
+    square(0, 3)
 
     loads[8].wait()
     loads[9].wait()
@@ -216,18 +216,15 @@
         own = own * shifted(own, 1 << (level - 1))
         own_factors.append(jnp.where(step_row >= (1 << level), own, 0.0))
 
-    loads[5].wait()
-    kh[...], kl[...] = split(raw[1])
-
 
     for copy in sums:
         copy.wait()
-    information = part_in[0]
+    driving = part_in[0]
     for i in range(1, nc):
-        information = information + part_in[i]
-    drive[x] = times(information, kh[...], kl[...])
+        driving = driving + part_in[i]
+    drive[x] = driving
     spread = []
-    for i in range(1, nx):
+    for i in far_first(nx):
         copy = remote(drive.at[x], drive.at[x], x_send.at[i], x_recv.at[i], x_peer(i))
         copy.start()
         spread.append(copy)
@@ -236,6 +233,8 @@
         widened(0)
     if len(rounds) > 1:
         widen(1)
+    square(3, 4)
+    fgh[1 - core, 0], fgl[1 - core, 0] = split(raw[2 * (1 - core)])
     loads[7].wait()
     th, tl = split(raw[3])
     eye = lax.broadcasted_iota(jnp.int32, (width, width), 0) == lax.broadcasted_iota(
@@ -244,7 +243,6 @@
     product = dot(th, gh[0]) + (dot(th, gl[0]) + dot(tl, gh[0]))
     wh[...], wl[...] = split(jnp.where(eye, 1.0, 0.0) - product)
     take_powers(0, 4)
-    square(4, 5)
 
     for copy in spread:
         copy.wait()
@@ -258,12 +256,12 @@
     ends[z] = local[span - 1 :]
     fbuf[...] = local.reshape(nx, steps, width)
     across = []
-    for i in sorted(range(1, nz), key=lambda i: -min(i, nz - i)):
+    for i in far_first(nz):
         copy = remote(ends.at[z], ends.at[z], e_send.at[i], e_recv.at[i], z_peer(i))
         copy.start()
         across.append(copy)
 
-    square(5, local_bits + z_bits - 1)
+    square(4, local_bits + z_bits - 2)
 
     last_plane = z == nz - 1
     corrected = times(local, wh[...], wl[...])
@@ -276,11 +274,12 @@
     for level in range(local_bits - 1, 2, -1):
         backward = backward + times(shifted(backward, -(1 << level)), gh[level], gl[level])
     starts[z] = backward[:1]
-    for i in sorted(range(1, nz), key=lambda i: -min(i, nz - i)):
+    for i in far_first(nz):
         copy = remote(starts.at[z], starts.at[z], b_send.at[i], b_recv.at[i], z_peer(i))
         copy.start()
         across.append(copy)
 
+    square(local_bits + z_bits - 2, local_bits + z_bits - 1)
     take_powers(4, local_bits + z_bits - 1)
 
     for copy in across[: nz - 1]:
@@ -306,7 +305,7 @@
         copies = []
         for k in range(width // BLOCK):
             out[k] = state[:, k * BLOCK : (k + 1) * BLOCK]
-        for i in range(1, nc):
+        for i in far_first(nc):
             there = lax.rem(chan + i, nc)
             copy = remote(out.at[there // 2], into.at[chan], send.at[i], recv.at[i], chan_peer(i))
             copy.start()
@@ -400,8 +399,6 @@
                 pltpu.VMEM((4, *square), f32),
                 pltpu.VMEM((2, powers, *square), bf16),
                 pltpu.VMEM((2, powers, *square), bf16),
-                pltpu.VMEM(square, bf16),
-                pltpu.VMEM(square, bf16),
                 pltpu.VMEM(square, bf16),
                 pltpu.VMEM(square, bf16),
                 pltpu.VMEM((powers - 1, *square), f32),

time: 47.7 us -> 46.7 us (0.979)
  Pallas kernels: 45.3 us -> 44.3 us
    pallas_call x1, Pallas kernels: 45.3 us -> 44.3 us  [per_device(): pl.pallas_call(functools.partial(kernel, nx, nz, nc, steps, width, channe...]
where the time goes in v5:
time: 46.7 us; the launch traced here: 46.5 us
  Pallas kernels  44.3 us (95%)
  other arithmetic  1.56 us (3%)
  between operations  0.65 us (1%)
    pallas_call x1, Pallas kernels, per_device(): pl.pallas_call(functools.partial(kernel, nx, nz, nc, steps, width, channe...  44.3 us
    select_n x1, other arithmetic, per_device(): jnp.where(odd, array[:, :, half:], array[:, :, :half])  1.56 us

profile of v5, /device:TPU:1, one launch (start us, length us, event | category | flops | bytes accessed | tf_op | source)
XLA Modules:
  0.0 46.5 jit_solution(17929182616536562288)
XLA Ops:
  0.6 44.3 %shard_map.113 = (f32[8,8,128]{2,1,0:T(8,128)}, f32[8,8,128]{2,1,0:T(8,128)}) custom-call(bf16[8,8,512]{2,1,0:T(8,128)(2,1)} %obs_hbm.1, bf16[512,512]{1,0:T(8,128)(2,1)} %mat_hbm.1, s32[4,4]{1,0:T(4,128)} %pattern_hbm.1, f32[1,512]{1,0:T(1,128)} %bitcast.2, f32[8,512]{1,0:T(8,128)} %retention_hbm.1, f32[1,512]{1,0:T(1,128)} %bitcast.3, f32[512,512]{1,0:T(8,128)} %f_hbm.1, ...), custom_call_target="tpu_custom_call" | custom-call | tf_op jit(solution)/shard_map/pallas_call | solution.py:387
  45.0 1.6 %slice_select_fusion = (f32[8,8,64]{2,1,0:T(8,128)}, f32[8,8,64]{2,1,0:T(8,128)}) fusion(f32[8,8,128]{2,1,0:T(8,128)} %get-tuple-element.5, pred[]{:T(512)S(6)} %eq.3, f32[8,8,128]{2,1,0:T(8,128)} %get-tuple-element.4), kind=kLoop, calls=%fused_computation | loop fusion | flops 8192 | bytes 98305 | tf_op jit(solution)/shard_map/jit(_where)/select_n | solution.py:441

commit v6 on v5

--- a/solution.py
+++ b/solution.py
@@ -111,6 +111,13 @@
     def widened(k):
         pl.semaphore_wait(ready.at[k], len(ring(rounds[k])))
 
+    sent = []
+
+    def landed(copies):
+        for copy in reversed(copies):
+            copy.wait_recv()
+        sent.extend(copies)
+
     def far_first(count):
         return sorted(range(1, count), key=lambda i: -min(i, count - i))
 
@@ -217,8 +224,7 @@
         own_factors.append(jnp.where(step_row >= (1 << level), own, 0.0))
 
 
-    for copy in sums:
-        copy.wait()
+    landed(sums)
     driving = part_in[0]
     for i in range(1, nc):
         driving = driving + part_in[i]
@@ -244,8 +250,7 @@
     wh[...], wl[...] = split(jnp.where(eye, 1.0, 0.0) - product)
     take_powers(0, 4)
 
-    for copy in spread:
-        copy.wait()
+    landed(spread)
     if len(rounds) > 1:
         widened(1)
 
@@ -280,13 +285,14 @@
         across.append(copy)
 
     square(local_bits + z_bits - 2, local_bits + z_bits - 1)
-    take_powers(4, local_bits + z_bits - 1)
-
-    for copy in across[: nz - 1]:
-        copy.wait()
+    take_powers(4, local_bits + z_bits - 2)
+
+    landed(across[: nz - 1])
 
     carry = jnp.where(block_row == 0, prior[...], shifted(ends[...].reshape(nz, width), 1))
     for level in range(z_bits):
+        if level == z_bits - 1:
+            take_powers(local_bits + z_bits - 2, local_bits + z_bits - 1)
         moved = shifted(carry, 1 << level)
         high, low = fh[local_bits + level], fl[local_bits + level]
         carry = carry + block_factors[level] * times(moved, high, low)
@@ -313,7 +319,6 @@
         into[chan] = out[chan // 2]
         return copies
 
-    copies_f = send_out(fbuf[x] + own_rows(rows_y), out_f, in_f, of_send, of_recv)
 
     rows_c[...] = times(rows_y[...], wh[...], wl[...])
     rows_c[total - 1 :] = rows_y[total - 1 :]
@@ -323,8 +328,8 @@
         half = nx * nz << level
         rows_c[:half] = rows_c[:half] + times(rows_c[half : 2 * half], gh[level], gl[level])
 
-    for copy in across[nz - 1 :]:
-        copy.wait()
+    copies_f = send_out(fbuf[x] + own_rows(rows_y), out_f, in_f, of_send, of_recv)
+    landed(across[nz - 1 :])
     whole = block_row == z
     for q in range(nx):
         own_start = bbuf[q][:1]
@@ -357,11 +362,12 @@
         state = state + times(moved, gh[level], gl[level])
     copies_s = send_out(state, out_s, in_s, os_send, os_recv)
 
+    for copy in sent + copies_f + copies_s:
+        copy.wait_send()
     for i in range(local_bits + z_bits - 1):
         power_copy(i).wait_send()
     for copies, into, result in ((copies_f, in_f, filtered), (copies_s, in_s, smoothed)):
-        for copy in copies:
-            copy.wait()
+        landed(copies)
         result[...] = into[...]
 
 

time: 46.7 us -> 45.8 us (0.981)
  Pallas kernels: 44.3 us -> 43.4 us
    pallas_call x1, Pallas kernels: 44.3 us -> 43.4 us  [per_device(): pl.pallas_call(functools.partial(kernel, nx, nz, nc, steps, width, channe...]
where the time goes in v6:
time: 45.8 us; the launch traced here: 45.6 us
  Pallas kernels  43.4 us (95%)
  other arithmetic  1.56 us (3%)
  between operations  0.65 us (1%)
    pallas_call x1, Pallas kernels, per_device(): pl.pallas_call(functools.partial(kernel, nx, nz, nc, steps, width, channe...  43.4 us
    select_n x1, other arithmetic, per_device(): jnp.where(odd, array[:, :, half:], array[:, :, :half])  1.56 us

profile of v6, /device:TPU:1, one launch (start us, length us, event | category | flops | bytes accessed | tf_op | source)
XLA Modules:
  0.0 45.6 jit_solution(6636852440361595965)
XLA Ops:
  0.6 43.4 %shard_map.113 = (f32[8,8,128]{2,1,0:T(8,128)}, f32[8,8,128]{2,1,0:T(8,128)}) custom-call(bf16[8,8,512]{2,1,0:T(8,128)(2,1)} %obs_hbm.1, bf16[512,512]{1,0:T(8,128)(2,1)} %mat_hbm.1, s32[4,4]{1,0:T(4,128)} %pattern_hbm.1, f32[1,512]{1,0:T(1,128)} %bitcast.2, f32[8,512]{1,0:T(8,128)} %retention_hbm.1, f32[1,512]{1,0:T(1,128)} %bitcast.3, f32[512,512]{1,0:T(8,128)} %f_hbm.1, ...), custom_call_target="tpu_custom_call" | custom-call | tf_op jit(solution)/shard_map/pallas_call | solution.py:393
  44.1 1.6 %slice_select_fusion = (f32[8,8,64]{2,1,0:T(8,128)}, f32[8,8,64]{2,1,0:T(8,128)}) fusion(f32[8,8,128]{2,1,0:T(8,128)} %get-tuple-element.5, pred[]{:T(512)S(6)} %eq.3, f32[8,8,128]{2,1,0:T(8,128)} %get-tuple-element.4), kind=kLoop, calls=%fused_computation | loop fusion | flops 8192 | bytes 98305 | tf_op jit(solution)/shard_map/jit(_where)/select_n | solution.py:447

commit v7 on v6

--- a/solution.py
+++ b/solution.py
@@ -248,7 +248,7 @@
     )
     product = dot(th, gh[0]) + (dot(th, gl[0]) + dot(tl, gh[0]))
     wh[...], wl[...] = split(jnp.where(eye, 1.0, 0.0) - product)
-    take_powers(0, 4)
+    take_powers(0, local_bits - 2)
 
     landed(spread)
     if len(rounds) > 1:
@@ -256,6 +256,8 @@
 
     local = drive[...].reshape(span, width)
     for level in range(local_bits):
+        if level == local_bits - 1:
+            take_powers(local_bits - 2, local_bits - 1)
         moved = shifted(local, 1 << level)
         local = local + own_factors[level] * times(moved, fh[level], fl[level])
     ends[z] = local[span - 1 :]
@@ -285,7 +287,7 @@
         across.append(copy)
 
     square(local_bits + z_bits - 2, local_bits + z_bits - 1)
-    take_powers(4, local_bits + z_bits - 2)
+    take_powers(local_bits - 1, local_bits + z_bits - 2)
 
     landed(across[: nz - 1])
 

time: 45.8 us -> 46.1 us (level)
  no operation moved by 1% of the time
where the time goes in v7:
time: 46.1 us; the launch traced here: 45.9 us
  Pallas kernels  43.7 us (95%)
  other arithmetic  1.56 us (3%)
  between operations  0.65 us (1%)
    pallas_call x1, Pallas kernels, per_device(): pl.pallas_call(functools.partial(kernel, nx, nz, nc, steps, width, channe...  43.7 us
    select_n x1, other arithmetic, per_device(): jnp.where(odd, array[:, :, half:], array[:, :, :half])  1.56 us

profile of v7, /device:TPU:1, one launch (start us, length us, event | category | flops | bytes accessed | tf_op | source)
XLA Modules:
  0.0 45.9 jit_solution(359946050164877298)
XLA Ops:
  0.6 43.7 %shard_map.113 = (f32[8,8,128]{2,1,0:T(8,128)}, f32[8,8,128]{2,1,0:T(8,128)}) custom-call(bf16[8,8,512]{2,1,0:T(8,128)(2,1)} %obs_hbm.1, bf16[512,512]{1,0:T(8,128)(2,1)} %mat_hbm.1, s32[4,4]{1,0:T(4,128)} %pattern_hbm.1, f32[1,512]{1,0:T(1,128)} %bitcast.2, f32[8,512]{1,0:T(8,128)} %retention_hbm.1, f32[1,512]{1,0:T(1,128)} %bitcast.3, f32[512,512]{1,0:T(8,128)} %f_hbm.1, ...), custom_call_target="tpu_custom_call" | custom-call | tf_op jit(solution)/shard_map/pallas_call | solution.py:395
  44.3 1.6 %slice_select_fusion = (f32[8,8,64]{2,1,0:T(8,128)}, f32[8,8,64]{2,1,0:T(8,128)}) fusion(f32[8,8,128]{2,1,0:T(8,128)} %get-tuple-element.5, pred[]{:T(512)S(6)} %eq.3, f32[8,8,128]{2,1,0:T(8,128)} %get-tuple-element.4), kind=kLoop, calls=%fused_computation | loop fusion | flops 8192 | bytes 98305 | tf_op jit(solution)/shard_map/jit(_where)/select_n | solution.py:449

commit v8 on v7

--- a/solution.py
+++ b/solution.py
@@ -322,13 +322,19 @@
         return copies
 
 
-    rows_c[...] = times(rows_y[...], wh[...], wl[...])
+    scaled = rows_y[...].astype(bf16)
+    rows_c[...] = dot(scaled, wh[...]) + dot(scaled, wl[...])
     rows_c[total - 1 :] = rows_y[total - 1 :]
     own_corrected = cbuf[x] + own_rows(rows_c)
 
     for level in (2, 1, 0):
         half = nx * nz << level
-        rows_c[:half] = rows_c[:half] + times(rows_c[half : 2 * half], gh[level], gl[level])
+        upper = rows_c[half : 2 * half]
+        if half >= 256:
+            upper = upper.astype(bf16)
+            rows_c[:half] = rows_c[:half] + (dot(upper, gh[level]) + dot(upper, gl[level]))
+        else:
+            rows_c[:half] = rows_c[:half] + times(upper, gh[level], gl[level])
 
     copies_f = send_out(fbuf[x] + own_rows(rows_y), out_f, in_f, of_send, of_recv)
     landed(across[nz - 1 :])

time: 46.1 us -> 46 us (level)
  no operation moved by 1% of the time
where the time goes in v8:
time: 46 us; the launch traced here: 45.8 us
  Pallas kernels  43.6 us (95%)
  other arithmetic  1.56 us (3%)
  between operations  0.65 us (1%)
    pallas_call x1, Pallas kernels, per_device(): pl.pallas_call(functools.partial(kernel, nx, nz, nc, steps, width, channe...  43.6 us
    select_n x1, other arithmetic, per_device(): jnp.where(odd, array[:, :, half:], array[:, :, :half])  1.56 us

profile of v8, /device:TPU:1, one launch (start us, length us, event | category | flops | bytes accessed | tf_op | source)
XLA Modules:
  0.0 45.8 jit_solution(10181657335235091404)
XLA Ops:
  0.6 43.6 %shard_map.113 = (f32[8,8,128]{2,1,0:T(8,128)}, f32[8,8,128]{2,1,0:T(8,128)}) custom-call(bf16[8,8,512]{2,1,0:T(8,128)(2,1)} %obs_hbm.1, bf16[512,512]{1,0:T(8,128)(2,1)} %mat_hbm.1, s32[4,4]{1,0:T(4,128)} %pattern_hbm.1, f32[1,512]{1,0:T(1,128)} %bitcast.2, f32[8,512]{1,0:T(8,128)} %retention_hbm.1, f32[1,512]{1,0:T(1,128)} %bitcast.3, f32[512,512]{1,0:T(8,128)} %f_hbm.1, ...), custom_call_target="tpu_custom_call" | custom-call | tf_op jit(solution)/shard_map/pallas_call | solution.py:401
  44.3 1.6 %slice_select_fusion = (f32[8,8,64]{2,1,0:T(8,128)}, f32[8,8,64]{2,1,0:T(8,128)}) fusion(f32[8,8,128]{2,1,0:T(8,128)} %get-tuple-element.5, pred[]{:T(512)S(6)} %eq.3, f32[8,8,128]{2,1,0:T(8,128)} %get-tuple-element.4), kind=kLoop, calls=%fused_computation | loop fusion | flops 8192 | bytes 98305 | tf_op jit(solution)/shard_map/jit(_where)/select_n | solution.py:455
